TPU v7x, 512 devices: a whole 4x8x8 slice. The times are simulated.
512 devices in a mesh: dp: 128 (over z, x_hi, y), sub: 4 (over x_lo, core).
Axes of the slice: x: 4 (x_hi: 2, x_lo: 2; x = x_hi * 2 + x_lo), y: 8, z: 8, core: 2. Of those that a mesh axis runs over, the one named last changes fastest.
Arguments:
- queries: bfloat16 [65536, 3584], P(('dp', 'sub')), may hold values from -4 to 4
- passages: bfloat16 [65536, 3584], P(('dp', 'sub')), may hold values from -4 to 4
- requests: int32 [512, 128, 3], P(('dp', 'sub')), may hold values from 0 to 127, as said below
- counts: int32 [512, 128], P(('dp', 'sub')), may hold values from 1 to 3, as said below
- neg_slot: int32 [65536, 7], P(('dp', 'sub')), may hold values from 0 to 383, as said below
Outputs:
- question_derivative: bfloat16 [65536, 3584], P(('dp', 'sub'))
- passage_grad: bfloat16 [65536, 3584], P(('dp', 'sub'))
- loss: float32 [], replicated
Inputs may be any that keep to these rules, and one draw needn't show every extreme that they name: `requests`: rows asked of an owner, inside that owner's block. Slots c < counts[d, o] of owner o are live for device d. `neg_slot`: each row names 7 different live slots of its own device's table, slot t belonging to owner t // 3 and position t % 3.
All inputs are finite; a program needn't handle non-finite values.
Results may differ from a plain program's by a relative error of at most 0.0062.
Values may be sent and summed in bfloat16 or wider, within the bound.
A program may use at most 128 MiB of HBM per device.

v0:
```python
import jax
import jax.numpy as jnp
from jax import lax
from jax.sharding import PartitionSpec as P

SHIFTS = 4


SHARPNESS_FACTOR = 50.0
EPSILON = 1e-06


def passed_along(value, axis, steps):
    count = lax.axis_size(axis)
    pairs = [(source, (source + steps) % count) for source in range(count)]
    return lax.ppermute(value, axis, pairs)


def unit_rows(values):
    widened = values.astype(jnp.float32)
    lengths = jnp.sqrt(jnp.sum(widened * widened, axis=1, keepdims=True) + EPSILON)
    return (widened / lengths, lengths)


def project_back(grad, unit, lengths):
    radial = jnp.sum(unit * grad, axis=1, keepdims=True)
    return ((grad - unit * radial) / lengths).astype(jnp.bfloat16)


def on_device(queries, passages, requests, counts, neg_slot):
    row_count = queries.shape[0]
    owners = requests.shape[1]
    slot_cap = requests.shape[2]
    slot_count = owners * slot_cap
    query_unit, query_len = unit_rows(queries)
    passage_unit, passage_len = unit_rows(passages)
    question_reduced_precision = query_unit.astype(jnp.bfloat16)
    passage_bf = passage_unit.astype(jnp.bfloat16)
    asked_rows = lax.all_to_all(requests[0], "dp", split_axis=0, concat_axis=0, tiled=True).reshape(
        slot_count
    )
    wanted = jnp.take(passage_bf, asked_rows, axis=0).reshape(owners, slot_cap, -1)
    retrieved_distractors = lax.all_to_all(
        wanted, "dp", split_axis=0, concat_axis=0, tiled=True
    ).reshape(slot_count, -1)
    section_sequence = [passage_bf]
    for offset in range(1, SHIFTS):
        section_sequence.append(passed_along(section_sequence[-1], "dp", 1))
    slot_ids = jnp.arange(slot_count, dtype=jnp.int32)
    live_slot = slot_ids % slot_cap < jnp.repeat(counts[0], slot_cap)
    chosen = jnp.sum((neg_slot[:, :, None] == slot_ids[None, None, :]).astype(jnp.float32), axis=1)
    distractor_indicator = chosen * live_slot.astype(jnp.float32)[None, :]
    section_similarity_scores = [
        SHARPNESS_FACTOR
        * jnp.dot(
            question_reduced_precision, document_section.T, preferred_element_type=jnp.float32
        )
        for document_section in section_sequence
    ]
    powers = [jnp.exp(logit) for logit in section_similarity_scores]
    distractor_exponentials = (
        jnp.exp(
            SHARPNESS_FACTOR
            * jnp.dot(
                question_reduced_precision,
                retrieved_distractors.T,
                preferred_element_type=jnp.float32,
            )
        )
        * distractor_indicator
    )
    totals = jnp.sum(distractor_exponentials, axis=1)
    for power in powers:
        totals = totals + jnp.sum(power, axis=1)
    loss_part = jnp.sum(jnp.log(totals) - jnp.diagonal(section_similarity_scores[0]))
    identity = jnp.eye(row_count, dtype=jnp.float32)
    distractor_importance = (distractor_exponentials / totals[:, None]).astype(jnp.bfloat16)
    question_derivative = jnp.dot(
        distractor_importance, retrieved_distractors, preferred_element_type=jnp.float32
    )
    normalized_probabilities = []
    for offset in range(SHIFTS):
        scaled = powers[offset] / totals[:, None]
        if offset == 0:
            scaled = scaled - identity
        normalized_probabilities.append(scaled.astype(jnp.bfloat16))
        question_derivative = question_derivative + jnp.dot(
            normalized_probabilities[offset],
            section_sequence[offset],
            preferred_element_type=jnp.float32,
        )
    question_derivative = SHARPNESS_FACTOR * question_derivative

    def section_objective_piece(offset):
        return SHARPNESS_FACTOR * jnp.dot(
            normalized_probabilities[offset].T,
            question_reduced_precision,
            preferred_element_type=jnp.float32,
        )

    summed = section_objective_piece(0)
    for offset in range(1, SHIFTS):
        summed = section_objective_piece(offset) + passed_along(summed, "dp", 1)
    summed = passed_along(summed, "dp", 1 - SHIFTS)
    sent_sums = (
        SHARPNESS_FACTOR
        * jnp.dot(
            distractor_importance.T, question_reduced_precision, preferred_element_type=jnp.float32
        )
    ).astype(jnp.bfloat16)
    returned = lax.all_to_all(
        sent_sums.reshape(owners, slot_cap, -1), "dp", split_axis=0, concat_axis=0, tiled=True
    ).reshape(slot_count, -1)
    pick_rows = (asked_rows[:, None] == jnp.arange(row_count, dtype=jnp.int32)[None, :]).astype(
        jnp.bfloat16
    )
    passage_grad = summed + jnp.dot(pick_rows.T, returned, preferred_element_type=jnp.float32)
    loss_total = lax.psum(loss_part, ("dp", "sub"))
    pair_count = row_count * lax.axis_size("dp") * lax.axis_size("sub")
    return (
        project_back(question_derivative, query_unit, query_len),
        project_back(passage_grad, passage_unit, passage_len),
        loss_total / pair_count,
    )


def solution(mesh):
    placed = (
        P(("dp", "sub"), None),
        P(("dp", "sub"), None),
        P(("dp", "sub"), None, None),
        P(("dp", "sub"), None),
        P(("dp", "sub"), None),
    )
    return jax.shard_map(
        on_device,
        mesh=mesh,
        in_specs=placed,
        out_specs=(P(("dp", "sub"), None), P(("dp", "sub"), None), P()),
        check_vma=False,
    )
```

profile of v0, /device:TPU:1, one launch (start us, length us, event | category | flops | bytes accessed | tf_op | source)
XLA Modules:
  0.0 698.8 jit_solution(4753255660074887809)
XLA Ops:
  2.0 20.8 %all-to-all-start = ((s32[128,1,3]{2,1,0:T(1,128)}), s32[128,1,3]{2,1,0:T(1,128)S(1)}, u32[]{:S(2)}, u32[]{:S(2)}) async-start(s32[128,1,3]{2,1,0:T(1,128)} %copy.24), calls=%async_computation | async-start | bytes 131072 | tf_op jit(solution)/shard_map/all_to_all | solution.py:39
  25.7 10.1 %all-to-all-done = s32[128,1,3]{2,1,0:T(1,128)S(1)} async-done(((s32[128,1,3]{2,1,0:T(1,128)}), s32[128,1,3]{2,1,0:T(1,128)S(1)}, u32[]{:S(2)}, u32[]{:S(2)}) %all-to-all-start) | async-done | bytes 1568 | tf_op jit(solution)/shard_map/all_to_all | solution.py:39
  37.4 3.9 gather_fusion
  41.2 6.7 gather.11
  48.2 5.7 broadcast_select_fusion
  53.9 7.4 %all-to-all-start.1 = ((bf16[128,3,3584]{2,1,0:T(4,128)(2,1)}), bf16[128,3,3584]{2,1,0:T(4,128)(2,1)}, u32[]{:S(2)}, u32[]{:S(2)}) async-start(bf16[128,3,3584]{2,1,0:T(4,128)(2,1)} %broadcast_select_fusion), calls=%async_computation.1 | async-start | bytes 7340032 | tf_op jit(solution)/shard_map/all_to_all | solution.py:43
  61.3 2.3 collective-permute-start
  63.9 101.2 %collective-permute-done = bf16[128,3584]{1,0:T(8,128)(2,1)S(1)} collective-permute-done((bf16[128,3584]{1,0:T(8,128)(2,1)S(1)}, bf16[128,3584]{1,0:T(8,128)(2,1)S(1)}, u32[]{:S(2)}, u32[]{:S(2)}) %collective-permute-start) | collective-permute-done | bytes 917536 | tf_op jit(solution)/shard_map/ppermute | solution.py:16
  167.7 24.6 %collective-permute-done.1 = bf16[128,3584]{1,0:T(8,128)(2,1)} collective-permute-done((bf16[128,3584]{1,0:T(8,128)(2,1)S(1)}, bf16[128,3584]{1,0:T(8,128)(2,1)}, u32[]{:S(2)}, u32[]{:S(2)}) %collective-permute-start.1) | collective-permute-done | bytes 917536 | tf_op jit(solution)/shard_map/ppermute | solution.py:16
  199.3 19.6 %collective-permute-done.2 = bf16[128,3584]{1,0:T(8,128)(2,1)} collective-permute-done((bf16[128,3584]{1,0:T(8,128)(2,1)}, bf16[128,3584]{1,0:T(8,128)(2,1)}, u32[]{:S(2)}, u32[]{:S(2)}) %collective-permute-start.2) | collective-permute-done | bytes 917536 | tf_op jit(solution)/shard_map/ppermute | solution.py:16
  220.4 7.1 %reshape.119 = bf16[384,3584]{1,0:T(8,128)(2,1)} reshape(bf16[128,3,3584]{2,1,0:T(4,128)(2,1)} %all-to-all-done.1) | data formatting | bytes 5505024 | tf_op jit(solution)/shard_map/reshape | solution.py:45
  227.5 2.8 fusion.24
  234.7 2.5 fusion
  237.2 6.7 reshape.122
  243.9 11.2 %all-to-all-start.2 = ((bf16[128,3,3584]{2,1,0:T(4,128)(2,1)}), bf16[128,3,3584]{2,1,0:T(4,128)(2,1)}, u32[]{:S(2)}, u32[]{:S(2)}) async-start(bf16[128,3,3584]{2,1,0:T(4,128)(2,1)} %reshape.122), calls=%async_computation.2 | async-start | bytes 7340032 | tf_op jit(solution)/shard_map/all_to_all | solution.py:111
  255.2 60.2 %collective-permute-done.3 = f32[128,3584]{1,0:T(8,128)} collective-permute-done((f32[128,3584]{1,0:T(8,128)}, f32[128,3584]{1,0:T(8,128)}, u32[]{:S(2)}, u32[]{:S(2)}) %collective-permute-start.3) | collective-permute-done | bytes 1835040 | tf_op jit(solution)/shard_map/ppermute | solution.py:16
  319.6 99.2 %collective-permute-done.4 = f32[128,3584]{1,0:T(8,128)S(1)} collective-permute-done((f32[128,3584]{1,0:T(8,128)S(1)}, f32[128,3584]{1,0:T(8,128)S(1)}, u32[]{:S(2)}, u32[]{:S(2)}) %collective-permute-start.4) | collective-permute-done | bytes 1835040 | tf_op jit(solution)/shard_map/ppermute | solution.py:16
  426.5 38.0 %collective-permute-done.5 = f32[128,3584]{1,0:T(8,128)} collective-permute-done((f32[128,3584]{1,0:T(8,128)}, f32[128,3584]{1,0:T(8,128)}, u32[]{:S(2)}, u32[]{:S(2)}) %collective-permute-start.5) | collective-permute-done | bytes 1835040 | tf_op jit(solution)/shard_map/ppermute | solution.py:16
  464.5 3.1 add.123
  469.5 2.9 convolution_add_fusion.1
  472.3 207.7 %psum.7 = f32[]{:T(128)} all-reduce(f32[]{:T(128)} %get-tuple-element.3), channel_id=1, replica_groups=mesh['dp'=128,'sub'=4] {'dp','sub'}, use_global_device_ids=true, to_apply=%region_11.12 | all-reduce | flops 1 | bytes 8 | tf_op jit(solution)/shard_map/psum | solution.py:118
  680.7 2.4 multiply_reduce_fusion.1
  684.5 7.1 %reshape.123 = bf16[384,3584]{1,0:T(8,128)(2,1)} reshape(bf16[128,3,3584]{2,1,0:T(4,128)(2,1)} %all-to-all-done.2) | data formatting | bytes 5505024 | tf_op jit(solution)/shard_map/reshape | solution.py:113
  691.6 2.6 fusion.10
  (61 shorter events, 40.3 us)
Async XLA Ops:
  2.0 33.8 %all-to-all-start = ((s32[128,1,3]{2,1,0:T(1,128)}), s32[128,1,3]{2,1,0:T(1,128)S(1)}, u32[]{:S(2)}, u32[]{:S(2)}) async-start(s32[128,1,3]{2,1,0:T(1,128)} %copy.24), calls=%async_computation | async-start | bytes 131072 | tf_op jit(solution)/shard_map/all_to_all | solution.py:39
  53.9 9.8 %copy-start.2 = (bf16[128,3584]{1,0:T(8,128)(2,1)S(1)}, bf16[128,3584]{1,0:T(8,128)(2,1)}, u32[]{:S(2)}) copy-start(bf16[128,3584]{1,0:T(8,128)(2,1)} %param.5) | copy-start | bytes 2752516
  53.9 166.6 %all-to-all-start.1 = ((bf16[128,3,3584]{2,1,0:T(4,128)(2,1)}), bf16[128,3,3584]{2,1,0:T(4,128)(2,1)}, u32[]{:S(2)}, u32[]{:S(2)}) async-start(bf16[128,3,3584]{2,1,0:T(4,128)(2,1)} %broadcast_select_fusion), calls=%async_computation.1 | async-start | bytes 7340032 | tf_op jit(solution)/shard_map/all_to_all | solution.py:43
  61.3 103.8 %collective-permute-start = (bf16[128,3584]{1,0:T(8,128)(2,1)S(1)}, bf16[128,3584]{1,0:T(8,128)(2,1)S(1)}, u32[]{:S(2)}, u32[]{:S(2)}) collective-permute-start(bf16[128,3584]{1,0:T(8,128)(2,1)S(1)} %fusion.20), channel_id=1, source_target_pairs={{0,4},{4,8},{8,12},{12,16},{16,20},{20,24},{24,28},{28,32},{32,36}... | collective-permute-start | bytes 2752520 | tf_op jit(solution)/shard_map/ppermute | solution.py:16
  63.9 130.3 %copy-start.6 = (s32[1,128]{1,0:T(1,128)S(1)}, s32[1,128]{1,0:T(1,128)}, u32[]{:S(2)}) copy-start(s32[1,128]{1,0:T(1,128)} %param.8) | copy-start | bytes 1540
  63.9 131.9 %copy-start.5 = (s32[128,7]{0,1:T(8,128)S(1)}, s32[128,7]{0,1:T(8,128)}, u32[]{:S(2)}) copy-start(s32[128,7]{0,1:T(8,128)} %param.9) | copy-start | bytes 10756
  165.1 2.6 copy-start.3
  165.1 27.2 %collective-permute-start.1 = (bf16[128,3584]{1,0:T(8,128)(2,1)S(1)}, bf16[128,3584]{1,0:T(8,128)(2,1)}, u32[]{:S(2)}, u32[]{:S(2)}) collective-permute-start(bf16[128,3584]{1,0:T(8,128)(2,1)S(1)} %collective-permute-done), channel_id=1, source_target_pairs={{0,4},{4,8},{8,12},{12,16},{16,20},{20,24},{24,28},{28,32},{32,36}... | collective-permute-start | bytes 2752520 | tf_op jit(solution)/shard_map/ppermute | solution.py:16
  192.3 26.5 %collective-permute-start.2 = (bf16[128,3584]{1,0:T(8,128)(2,1)}, bf16[128,3584]{1,0:T(8,128)(2,1)}, u32[]{:S(2)}, u32[]{:S(2)}) collective-permute-start(bf16[128,3584]{1,0:T(8,128)(2,1)} %collective-permute-done.1), channel_id=1, source_target_pairs={{0,4},{4,8},{8,12},{12,16},{16,20},{20,24},{24,28},{28,32},{32,36}... | collective-permute-start | bytes 2752520 | tf_op jit(solution)/shard_map/ppermute | solution.py:16
  232.6 82.8 %collective-permute-start.3 = (f32[128,3584]{1,0:T(8,128)}, f32[128,3584]{1,0:T(8,128)}, u32[]{:S(2)}, u32[]{:S(2)}) collective-permute-start(f32[128,3584]{1,0:T(8,128)} %convolution_multiply_fusion.1), channel_id=1, source_target_pairs={{0,4},{4,8},{8,12},{12,16},{16,20},{20,24},{24,28},{28,32},{32,36}... | collective-permute-start | bytes 5505032 | tf_op jit(solution)/shard_map/ppermute | solution.py:16
  243.9 440.6 %all-to-all-start.2 = ((bf16[128,3,3584]{2,1,0:T(4,128)(2,1)}), bf16[128,3,3584]{2,1,0:T(4,128)(2,1)}, u32[]{:S(2)}, u32[]{:S(2)}) async-start(bf16[128,3,3584]{2,1,0:T(4,128)(2,1)} %reshape.122), calls=%async_computation.2 | async-start | bytes 7340032 | tf_op jit(solution)/shard_map/all_to_all | solution.py:111
  317.2 101.5 %collective-permute-start.4 = (f32[128,3584]{1,0:T(8,128)S(1)}, f32[128,3584]{1,0:T(8,128)S(1)}, u32[]{:S(2)}, u32[]{:S(2)}) collective-permute-start(f32[128,3584]{1,0:T(8,128)S(1)} %fusion.1), channel_id=1, source_target_pairs={{0,4},{4,8},{8,12},{12,16},{16,20},{20,24},{24,28},{28,32},{32,36}... | collective-permute-start | bytes 5505032 | tf_op jit(solution)/shard_map/ppermute | solution.py:16
  420.2 44.3 %collective-permute-start.5 = (f32[128,3584]{1,0:T(8,128)}, f32[128,3584]{1,0:T(8,128)}, u32[]{:S(2)}, u32[]{:S(2)}) collective-permute-start(f32[128,3584]{1,0:T(8,128)} %add.122), channel_id=1, source_target_pairs={{0,4},{4,8},{8,12},{12,16},{16,20},{20,24},{24,28},{28,32},{32,36}... | collective-permute-start | bytes 5505032 | tf_op jit(solution)/shard_map/ppermute | solution.py:16
  422.4 1.8 copy-start
  424.8 1.2 copy-start.4
  467.6 226.6 %collective-permute-start.6 = (f32[128,3584]{1,0:T(8,128)}, f32[128,3584]{1,0:T(8,128)}, u32[]{:S(2)}, u32[]{:S(2)}) collective-permute-start(f32[128,3584]{1,0:T(8,128)} %add.123), channel_id=1, source_target_pairs={{0,500},{4,504},{8,508},{12,0},{16,4},{20,8},{24,12},{28,16},{32,2... | collective-permute-start | bytes 5505032 | tf_op jit(solution)/shard_map/ppermute | solution.py:16
  691.6 2.6 copy-start.1
where the time goes:
time: 701 us; the launch traced here: 699 us
  waiting for transfers between devices  353 us (50%)
  blocking collectives  208 us (30%)
  starting transfers between devices  53.4 us (8%)
  local copies, waits for them, and re-layouts  37.7 us (5%)
  matrix products  24.3 us (3%)
  other arithmetic  20.1 us (3%)
    ppermute x7, waiting for transfers between devices, passed_along(): return lax.ppermute(value, axis, pairs)  343 us
    psum x1, blocking collectives, on_device(): loss_total = lax.psum(loss_part, ('dp', 'sub'))  208 us
    all_to_all x1, starting transfers between devices, on_device(): lax.all_to_all(requests[0], 'dp', split_axis=0, concat_axis=0, tiled=True)  20.8 us
  transfers between devices with their start and end apart: 10, of which 7 were waited for; matrix products, arithmetic and copies ran while one was open for 6% of the time, Pallas kernels for 0%

commit v1 on v0

v1 whole, which is shorter than its diff:
```python
import functools

import jax
import jax.numpy as jnp
import numpy as np
from jax import lax
from jax.experimental import pallas as pl
from jax.experimental.pallas import tpu as pltpu
from jax.sharding import PartitionSpec as P

SHIFTS = 4
CAP = 3
SHARPNESS = 50.0
EPSILON = 1e-06
Z_SIZE = 8
TILE = 256
MESH = pl.DeviceIdType.MESH
F32 = jnp.float32
BF16 = jnp.bfloat16


def tables(nz, nw):
    slots = nz * nw * CAP
    z, w, c = np.meshgrid(np.arange(nz), np.arange(nw), np.arange(CAP), indexing="ij")
    slot = ((z * nw + w) * CAP + c).reshape(-1)
    to_w = np.zeros((2 * slots, 2 * slots), np.float32)
    to_z = np.zeros((2 * slots, 2 * slots), np.float32)
    for half in range(2):
        by_w = (((w * 2 + half) * nz + z) * CAP + c).reshape(-1)
        by_z = (((z * 2 + half) * nw + w) * CAP + c).reshape(-1)
        to_w[by_w, half * slots + slot] = 1
        to_z[by_z, by_w] = 1
    expand = np.zeros((slots, nz * nw), np.float32)
    expand[slot, (w * nz + z).reshape(-1)] = 1
    column = np.zeros((slots, 128), np.float32)
    column[slot, c.reshape(-1)] = 1
    swap = np.zeros((nz * nw, nz * nw), np.float32)
    zz, ww = np.meshgrid(np.arange(nz), np.arange(nw), indexing="ij")
    swap[(ww * nz + zz).reshape(-1), (zz * nw + ww).reshape(-1)] = 1
    spread = np.zeros((nz * nw, slots), np.float32)
    spread[slot // CAP, slot] = 1
    place = np.broadcast_to((np.arange(slots) % CAP).astype(np.float32), (8, slots))
    b = lambda v: jnp.asarray(np.ascontiguousarray(v), BF16)
    return (
        b(to_w),
        b(to_w.T),
        b(to_z),
        b(expand),
        jnp.asarray(column),
        b(swap),
        b(spread),
        jnp.asarray(np.ascontiguousarray(place)),
    )


def mm(a, b):
    return jnp.dot(a, b, preferred_element_type=F32)


def mm_nt(a, b):
    return lax.dot_general(a, b, (((1,), (1,)), ((), ())), preferred_element_type=F32)


def at(index, size):
    return pl.ds(pl.multiple_of(index * size, size), size)


class Exchange:
    def __init__(self, place, x, y, bufs, sems, to_w, to_w_t, to_z):
        self.nz, self.nw, self.z, self.w, self.sub = place
        self.x, self.y = x, y
        self.r0, self.w0, self.rw0, self.w1, self.r1, self.z1 = bufs
        self.zs, self.zr, self.ws, self.wr, self.ls = sems
        self.to_w, self.to_w_t, self.to_z = to_w, to_w_t, to_z
        self.half = x.shape[1] // 2
        self.quarter = self.half // 2
        self.slots = x.shape[0]
        self.zrows = self.nw * CAP
        self.wrows = 2 * self.nz * CAP

    def z_peer(self, k):
        return lax.rem(self.z + k, self.nz)

    def w_peer(self, k):
        return lax.rem(self.w + k, self.nw)

    def z_dev(self, t):
        return (t * self.nw + self.w, self.sub)

    def w_dev(self, t):
        return (self.z * self.nw + t, self.sub)

    def z0(self, to, frm):
        return pltpu.make_async_remote_copy(
            self.x.at[at(to, self.zrows), pl.ds(0, self.half)],
            self.r0.at[at(frm, self.zrows)],
            self.zs.at[0, to],
            self.zr.at[0, frm],
            device_id=self.z_dev(to),
            device_id_type=MESH,
        )

    def z1c(self, h, to, frm):
        rows = pl.ds(pl.multiple_of(to * 2 * self.zrows + h * self.zrows, self.zrows), self.zrows)
        return pltpu.make_async_remote_copy(
            self.z1.at[rows],
            self.y.at[at(frm, self.zrows), pl.ds(self.half + h * self.quarter, self.quarter)],
            self.zs.at[1 + h, to],
            self.zr.at[1 + h, frm],
            device_id=self.z_dev(to),
            device_id_type=MESH,
        )

    def wc(self, kind, to, frm):
        src, dst = ((self.w0, self.rw0), (self.w1, self.r1))[kind]
        return pltpu.make_async_remote_copy(
            src.at[at(to, self.wrows)],
            dst.at[at(frm, self.wrows)],
            self.ws.at[kind, to],
            self.wr.at[kind, frm],
            device_id=self.w_dev(to),
            device_id_type=MESH,
        )

    def own(self, which):
        if which == 0:
            return pltpu.make_async_copy(
                self.x.at[at(self.z, self.zrows), pl.ds(0, self.half)],
                self.r0.at[at(self.z, self.zrows)],
                self.ls.at[0],
            )
        if which in (1, 2):
            src, dst = ((self.w0, self.rw0), (self.w1, self.r1))[which - 1]
            return pltpu.make_async_copy(
                src.at[at(self.w, self.wrows)], dst.at[at(self.w, self.wrows)], self.ls.at[which]
            )
        h = which - 3
        rows = pl.ds(
            pl.multiple_of(self.z * 2 * self.zrows + h * self.zrows, self.zrows), self.zrows
        )
        return pltpu.make_async_copy(
            self.z1.at[rows],
            self.y.at[at(self.z, self.zrows), pl.ds(self.half + h * self.quarter, self.quarter)],
            self.ls.at[which],
        )

    def each_z(self, act):
        lax.fori_loop(1, self.nz, lambda k, n: (act(self.z_peer(k)), n)[1], 0)

    def each_w(self, act):
        lax.fori_loop(1, self.nw, lambda k, n: (act(self.w_peer(k)), n)[1], 0)

    def reorder_to_w(self, dst, src, first):
        step = self.slots // 2 if self.slots % 32 == 0 else self.slots
        left = src[:, pl.ds(first, self.quarter)]
        right = src[:, pl.ds(first + self.quarter, self.quarter)]

        def body(i, n):
            m = self.to_w.at[at(i, step)]
            dst[at(i, step), :] = (
                mm(m[:, pl.ds(0, self.slots)], left)
                + mm(m[:, pl.ds(self.slots, self.slots)], right)
            ).astype(BF16)
            return n

        lax.fori_loop(0, 2 * self.slots // step, body, 0)

    def start_left(self):
        self.each_z(lambda t: self.z0(t, self.z).start())
        self.own(0).start()

    def start_right(self):
        self.reorder_to_w(self.w1, self.x, self.half)
        self.each_w(lambda t: self.wc(1, t, self.w).start())
        self.own(2).start()

    def turn_left(self):
        self.own(0).wait()
        self.each_z(lambda t: self.z0(self.z, t).wait_recv())
        self.reorder_to_w(self.w0, self.r0, 0)
        self.each_w(lambda t: self.wc(0, t, self.w).start())
        self.own(1).start()

    def turn_right(self):
        self.own(2).wait()
        self.each_w(lambda t: self.wc(1, self.w, t).wait_recv())
        step = self.slots // 2 if self.slots % 32 == 0 else self.slots

        def body(i, n):
            self.z1[at(i, step), :] = mm(self.to_z[at(i, step), :], self.r1[...]).astype(BF16)
            return n

        lax.fori_loop(0, 2 * self.slots // step, body, 0)
        for h in range(2):
            self.each_z(lambda t: self.z1c(h, t, self.z).start())
            self.own(3 + h).start()

    def end_left(self):
        self.own(1).wait()
        self.each_w(lambda t: self.wc(0, self.w, t).wait_recv())
        for h in range(2):
            self.y[:, pl.ds(h * self.quarter, self.quarter)] = mm(
                self.to_w_t[pl.ds(h * self.slots, self.slots), :], self.rw0[...]
            ).astype(BF16)

    def end_right(self):
        for h in range(2):
            self.own(3 + h).wait()
            self.each_z(lambda t: self.z1c(h, self.z, t).wait_recv())

    def drain(self):
        self.each_z(lambda t: self.z0(t, self.z).wait_send())
        for kind in range(2):
            self.each_w(lambda t: self.wc(kind, t, self.w).wait_send())
        for h in range(2):
            self.each_z(lambda t: self.z1c(h, t, self.z).wait_send())


def kernel(
    nz,
    nw,
    ns,
    q_ref,
    p_ref,
    req_ref,
    cnt_ref,
    neg_ref,
    to_w,
    to_w_t,
    to_z,
    expand,
    column,
    swap,
    spread,
    place,
    dq_ref,
    dp_ref,
    loss_ref,
    ask0,
    ask1,
    ask2,
    ask3,
    qb,
    pb,
    qlen,
    plen,
    ps,
    qs,
    x1,
    y1,
    x2,
    y2,
    bufs1,
    bufs2,
    power,
    wrow,
    wt,
    wt_in,
    hard_w,
    pick,
    pick_t,
    gq,
    gp,
    l1,
    l2,
    l3,
    az_s,
    az_r,
    aw_s,
    aw_r,
    sh_s,
    sh_r,
    zs,
    zr,
    ws,
    wr,
    ls,
    wt_s,
    wt_r,
    lz_s,
    lz_r,
    lw_s,
    lw_r,
    lsub_s,
    lsub_r,
):
    me = lax.axis_index("dp")
    sub = lax.axis_index("sub")
    ndp = nz * nw
    z, w = me // nw, lax.rem(me, nw)
    rows, depth = q_ref.shape
    slots = ndp * CAP
    tiles = depth // TILE
    spot = (nz, nw, z, w, sub)
    ex = [
        Exchange(
            spot,
            (x1, x2)[i],
            (y1, y2)[i],
            (bufs1, bufs2)[i],
            [s.at[i] for s in (zs, zr, ws, wr, ls)],
            to_w,
            to_w_t,
            to_z,
        )
        for i in range(2)
    ]
    along = ex[0]

    def dp_at(k):
        return lax.rem(me + (k + ndp), ndp)

    barrier = pltpu.get_barrier_semaphore()

    def greet(device):
        pl.semaphore_signal(barrier, inc=1, device_id=device, device_id_type=MESH)

    along.each_z(lambda t: greet(along.z_dev(t)))
    along.each_w(lambda t: greet(along.w_dev(t)))
    for k in range(1, SHIFTS):
        greet((dp_at(k), sub))
        greet((dp_at(-k), sub))

    def each_sub(act):
        lax.fori_loop(1, ns, lambda k, n: (act(lax.rem(sub + k, ns)), n)[1], 0)

    each_sub(lambda t: greet((me, t)))

    ask0[...] = jnp.zeros_like(ask0)
    ask0[:, pl.ds(0, CAP)] = req_ref[0].astype(F32)

    def unit(ref, out, length):
        total = jnp.zeros((rows, 1), F32)
        for i in range(tiles):
            v = ref[:, pl.ds(i * TILE, TILE)].astype(F32)
            total = total + jnp.sum(v * v, axis=1, keepdims=True)
        size = jnp.sqrt(total + EPSILON)
        length[...] = size
        for i in range(tiles):
            cols = pl.ds(i * TILE, TILE)
            out[:, cols] = (ref[:, cols].astype(F32) / size).astype(BF16)

    unit(p_ref, pb, plen)
    unit(q_ref, qb, qlen)
    pl.semaphore_wait(barrier, (nz - 1) + (nw - 1) + 2 * (SHIFTS - 1) + (ns - 1))

    def ask_z(to, frm):
        return pltpu.make_async_remote_copy(
            ask0.at[at(to, nw)], ask1.at[at(frm, nw)], az_s.at[to], az_r.at[frm],
            device_id=along.z_dev(to), device_id_type=MESH,
        )

    def ask_w(to, frm):
        return pltpu.make_async_remote_copy(
            ask2.at[at(to, nz)], ask3.at[at(frm, nz)], aw_s.at[to], aw_r.at[frm],
            device_id=along.w_dev(to), device_id_type=MESH,
        )

    def shift(k, side):
        own, held = ((pb, ps), (qb, qs))[side]
        return pltpu.make_async_remote_copy(
            own if k == 0 else held.at[k - 1],
            held.at[k],
            sh_s.at[side, k],
            sh_r.at[side, k],
            device_id=(dp_at(1 - 2 * side), sub),
            device_id_type=MESH,
        )

    along.each_z(lambda t: ask_z(t, z).start())
    for side in range(2):
        shift(0, side).start()
    ask1[at(z, nw), :] = ask0[at(z, nw), :]

    def logits(held):
        def body(i, total):
            cols = at(i, TILE)
            return total + mm_nt(qb[:, cols], held[:, cols])

        return SHARPNESS * lax.fori_loop(0, tiles, body, jnp.zeros((rows, rows), F32))

    along.each_z(lambda t: ask_z(z, t).wait_recv())
    ask2[...] = mm(swap[...], ask1[...].astype(BF16))
    along.each_w(lambda t: ask_w(t, w).start())
    ask3[at(w, nz), :] = ask2[at(w, nz), :]
    first = logits(pb)
    power[0] = jnp.exp(first)
    lane = lax.broadcasted_iota(jnp.int32, (rows, rows), 1)
    row = lax.broadcasted_iota(jnp.int32, (rows, rows), 0)
    eye = jnp.where(lane == row, 1.0, 0.0).astype(F32)
    diagonal = jnp.sum(first * eye, axis=1, keepdims=True)
    along.each_w(lambda t: ask_w(w, t).wait_recv())
    asked = mm(expand[...], ask3[...].astype(BF16))
    asked = jnp.sum(asked * column[...], axis=1, keepdims=True)
    picked = jnp.where(
        asked == lax.broadcasted_iota(jnp.int32, (slots, rows), 1).astype(F32), 1.0, 0.0
    ).astype(F32)
    pick[...] = picked.astype(BF16)
    pick_t[...] = picked.T.astype(BF16)

    half_tiles = tiles // 2

    def gather_rows(i, n):
        cols = at(i, TILE)
        x1[:, cols] = mm(pick[...], pb[:, cols]).astype(BF16)
        return n

    lax.fori_loop(0, half_tiles, gather_rows, 0)
    ex[0].start_left()
    lax.fori_loop(half_tiles, tiles, gather_rows, 0)
    ex[0].start_right()

    slot = lax.broadcasted_iota(jnp.int32, (rows, slots), 1)
    chosen = jnp.zeros((rows, slots), F32)
    for n in range(neg_ref.shape[1]):
        chosen = chosen + jnp.where(neg_ref[:, n : n + 1] == slot, 1.0, 0.0)
    limits = jnp.broadcast_to(cnt_ref[...].astype(F32), (8, ndp)).astype(BF16)
    live = jnp.where(place[...] < mm(limits, spread[...]), 1.0, 0.0)
    gq[:, pl.ds(0, slots)] = chosen * live[0:1]

    for side in range(2):
        shift(0, side).wait_recv()
        shift(1, side).start()
    power[1] = jnp.exp(logits(ps.at[0]))
    ex[0].turn_left()
    for side in range(2):
        shift(1, side).wait_recv()
        shift(2, side).start()
    power[2] = jnp.exp(logits(ps.at[1]))
    ex[0].turn_right()
    for side in range(2):
        shift(2, side).wait_recv()
    power[3] = jnp.exp(logits(ps.at[2]))
    ex[0].end_left()
    ex[0].end_right()

    def hard_logits(i, total):
        cols = at(i, TILE)
        return total + mm_nt(qb[:, cols], y1[:, cols])

    hard = lax.fori_loop(0, tiles, hard_logits, jnp.zeros((rows, slots), F32))
    hard = jnp.exp(SHARPNESS * hard) * gq[:, pl.ds(0, slots)]
    totals = jnp.sum(hard, axis=1, keepdims=True)
    for k in range(SHIFTS):
        totals = totals + jnp.sum(power[k], axis=1, keepdims=True)
    hard = hard / totals
    hard_w[...] = hard.astype(BF16)
    hard_t = hard.T.astype(BF16)

    def slot_sums(i, n):
        cols = at(i, TILE)
        x2[:, cols] = (SHARPNESS * mm(hard_t, qb[:, cols])).astype(BF16)
        return n

    lax.fori_loop(0, half_tiles, slot_sums, 0)
    ex[1].start_left()
    lax.fori_loop(half_tiles, tiles, slot_sums, 0)
    ex[1].start_right()

    def wt_copy(k):
        return pltpu.make_async_remote_copy(
            wt.at[k], wt_in.at[k - 1], wt_s.at[k - 1], wt_r.at[k - 1],
            device_id=(dp_at(-k), sub), device_id_type=MESH,
        )

    for k in range(SHIFTS):
        weight = power[k] / totals
        if k == 0:
            weight = weight - eye
        wrow[k] = weight.astype(BF16)
        wt[k] = weight.T.astype(BF16)
        if k:
            wt_copy(k).start()

    part = jnp.sum(jnp.log(totals) - diagonal)

    def lz(to, frm):
        return pltpu.make_async_remote_copy(
            l1.at[z], l1.at[frm], lz_s.at[to], lz_r.at[frm],
            device_id=along.z_dev(to), device_id_type=MESH,
        )

    def lw(to, frm):
        return pltpu.make_async_remote_copy(
            l2.at[w], l2.at[frm], lw_s.at[to], lw_r.at[frm],
            device_id=along.w_dev(to), device_id_type=MESH,
        )

    def lsub(to, frm):
        return pltpu.make_async_remote_copy(
            l3.at[sub], l3.at[frm], lsub_s.at[to], lsub_r.at[frm],
            device_id=(me, to), device_id_type=MESH,
        )

    def ordered_sum(ref):
        total = ref[0]
        for i in range(1, ref.shape[0]):
            total = total + ref[i]
        return total

    l1[pl.ds(z, 1)] = jnp.broadcast_to(part, (1, 8, 128))
    along.each_z(lambda t: lz(t, z).start())

    def project(raw, length, grad, out):
        size = length[...]

        def radial(i, total):
            cols = at(i, TILE)
            return total + jnp.sum(
                raw[:, cols].astype(F32) / size * grad[:, cols], axis=1, keepdims=True
            )

        along_unit = lax.fori_loop(0, tiles, radial, jnp.zeros((rows, 1), F32))

        def write(i, n):
            cols = at(i, TILE)
            u = raw[:, cols].astype(F32) / size
            out[:, cols] = ((grad[:, cols] - u * along_unit) / size).astype(BF16)
            return n

        lax.fori_loop(0, tiles, write, 0)

    def query_side(i, n):
        cols = at(i, TILE)
        total = mm(hard_w[...], y1[:, cols]) + mm(wrow[0], pb[:, cols])
        for k in range(1, SHIFTS):
            total = total + mm(wrow[k], ps[k - 1, :, cols])
        gq[:, cols] = SHARPNESS * total
        return n

    lax.fori_loop(0, tiles, query_side, 0)

    along.each_z(lambda t: lz(z, t).wait_recv())
    l2[pl.ds(w, 1)] = ordered_sum(l1)[None]
    along.each_w(lambda t: lw(t, w).start())

    project(q_ref, qlen, gq, dq_ref)

    ex[1].turn_left()

    for k in range(1, SHIFTS):
        wt_copy(k).wait_recv()

    def passage_side(i, n):
        cols = at(i, TILE)
        total = mm(wt[0], qb[:, cols])
        for k in range(1, SHIFTS):
            total = total + mm(wt_in[k - 1], qs[k - 1, :, cols])
        gp[:, cols] = SHARPNESS * total
        return n

    lax.fori_loop(0, tiles, passage_side, 0)
    along.each_w(lambda t: lw(w, t).wait_recv())
    l3[pl.ds(sub, 1)] = ordered_sum(l2)[None]
    each_sub(lambda t: lsub(t, sub).start())

    ex[1].turn_right()

    each_sub(lambda t: lsub(sub, t).wait_recv())
    loss_ref[...] = ordered_sum(l3) / float(rows * ndp * ns)

    ex[1].end_left()
    ex[1].end_right()

    def add_returned(i, n):
        cols = at(i, TILE)
        gp[:, cols] = gp[:, cols] + mm(pick_t[...], y2[:, cols])
        return n

    lax.fori_loop(0, tiles, add_returned, 0)
    project(p_ref, plen, gp, dp_ref)

    along.each_z(lambda t: ask_z(t, z).wait_send())
    along.each_w(lambda t: ask_w(t, w).wait_send())
    for k in range(SHIFTS - 1):
        for side in range(2):
            shift(k, side).wait_send()
    for k in range(1, SHIFTS):
        wt_copy(k).wait_send()
    along.each_z(lambda t: lz(t, z).wait_send())
    along.each_w(lambda t: lw(t, w).wait_send())
    each_sub(lambda t: lsub(t, sub).wait_send())
    for e in ex:
        e.drain()


def on_device(nz, nw, ns, queries, passages, requests, counts, neg_slot):
    rows, depth = queries.shape
    ndp = nz * nw
    slots = ndp * CAP
    half, quarter = depth // 2, depth // 4
    dma = pltpu.SemaphoreType.DMA
    v = pltpu.VMEM
    wide = lambda: [
        v((slots, half), BF16),
        v((2 * slots, quarter), BF16),
        v((2 * slots, quarter), BF16),
        v((2 * slots, quarter), BF16),
        v((2 * slots, quarter), BF16),
        v((2 * slots, quarter), BF16),
    ]
    n = SHIFTS - 1
    scratch = (
        [v((ndp, 128), F32)] * 4
        + [v((rows, depth), BF16)] * 2
        + [v((rows, 1), F32)] * 2
        + [v((n, rows, depth), BF16)] * 2
        + [v((slots, depth), BF16)] * 4
        + [wide(), wide()]
        + [v((SHIFTS, rows, rows), F32)]
        + [v((SHIFTS, rows, rows), BF16)] * 2
        + [v((n, rows, rows), BF16)]
        + [v((rows, slots), BF16), v((slots, rows), BF16), v((rows, slots), BF16)]
        + [v((rows, depth), F32)] * 2
        + [v((nz, 8, 128), F32), v((nw, 8, 128), F32), v((ns, 8, 128), F32)]
        + [dma((nz,)), dma((nz,)), dma((nw,)), dma((nw,))]
        + [dma((2, n)), dma((2, n))]
        + [dma((2, 3, nz)), dma((2, 3, nz)), dma((2, 2, nw)), dma((2, 2, nw)), dma((2, 5))]
        + [dma((n,)), dma((n,))]
        + [dma((nz,)), dma((nz,)), dma((nw,)), dma((nw,)), dma((ns,)), dma((ns,))]

    )
    vmem = pl.BlockSpec(memory_space=pltpu.VMEM)
    fixed = tables(nz, nw)
    flops = 2 * rows * depth * (SHIFTS * rows * 3 + slots * 5) + 14 * slots * slots * depth
    dq, dp, loss = pl.pallas_call(
        functools.partial(kernel, nz, nw, ns),
        out_shape=(
            jax.ShapeDtypeStruct((rows, depth), BF16),
            jax.ShapeDtypeStruct((rows, depth), BF16),
            jax.ShapeDtypeStruct((8, 128), F32),
        ),
        in_specs=[vmem] * (5 + len(fixed)),
        out_specs=(vmem, vmem, vmem),
        scratch_shapes=scratch,
        compiler_params=pltpu.CompilerParams(
            collective_id=0, has_side_effects=True, vmem_limit_bytes=60 << 20
        ),
        cost_estimate=pl.CostEstimate(
            flops=flops, bytes_accessed=12 * rows * depth, transcendentals=rows * slots * 2
        ),
    )(queries, passages, requests, counts, neg_slot, *fixed)
    return dq, dp, loss[0, 0]


def solution(mesh):
    ndp, ns = mesh.shape["dp"], mesh.shape["sub"]
    nz = Z_SIZE
    placed = (
        P(("dp", "sub"), None),
        P(("dp", "sub"), None),
        P(("dp", "sub"), None, None),
        P(("dp", "sub"), None),
        P(("dp", "sub"), None),
    )
    return jax.shard_map(
        functools.partial(on_device, nz, ndp // nz, ns),
        mesh=mesh,
        in_specs=placed,
        out_specs=(P(("dp", "sub"), None), P(("dp", "sub"), None), P()),
        check_vma=False,
    )
```

time: 701 us -> 261 us (0.37)
  the two profiles are of different devices: /device:TPU:1 before, /device:TPU:25 now
where the time goes in v1:
time: 261 us; the launch traced here: 260 us
  Pallas kernels  253 us (97%)
  local copies, waits for them, and re-layouts  7.19 us (3%)
    pallas_call x1, Pallas kernels, on_device(): pl.pallas_call(functools.partial(kernel, nz, nw, ns), out_shape=(jax.Shap...  253 us
    unnamed x6, local copies, waits for them, and re-layouts  5.92 us

profile of v1, /device:TPU:25, one launch (start us, length us, event | category | flops | bytes accessed | tf_op | source)
XLA Modules:
  0.0 260.4 jit_solution(10187574210217064437)
XLA Ops:
  0.6 1.4 copy.16.req_ref
  2.0 1.4 copy.17.neg_ref
  3.5 252.6 %shard_map.148 = (bf16[128,3584]{1,0:T(8,128)(2,1)}, bf16[128,3584]{1,0:T(8,128)(2,1)}, f32[8,128]{1,0:T(8,128)}) custom-call(bf16[128,3584]{1,0:T(8,128)(2,1)} %q_ref.1, bf16[128,3584]{1,0:T(8,128)(2,1)} %p_ref.1, s32[1,128,3]{2,1,0:T(8,128)} %copy.16.req_ref, s32[1,128]{1,0:T(1,128)} %cnt_ref.1, s32[128,7]{1,0:T(8,128)} %copy.17.neg_ref, ...), custom_call_target="tpu_custom_call" | custom-call | flops 10569646080 | bytes 5505024 | tf_op jit(solution)/shard_map/pallas_call | solution.py:626
  256.1 0.0 copy-start
  256.1 1.3 slice.3
  257.3 2.2 copy.20
  259.5 0.0 copy-done
  259.5 0.9 copy.21
Async XLA Ops:
  256.1 3.4 %copy-start = (bf16[128,3584]{1,0:T(8,128)(2,1)S(1)}, bf16[128,3584]{1,0:T(8,128)(2,1)}, u32[]{:S(2)}) copy-start(bf16[128,3584]{1,0:T(8,128)(2,1)} %get-tuple-element.13) | copy-start | bytes 2752516

commit v2 on v1

--- a/solution.py
+++ b/solution.py
@@ -14,6 +14,7 @@
 EPSILON = 1e-06
 Z_SIZE = 8
 TILE = 256
+WIDE = 512
 MESH = pl.DeviceIdType.MESH
 F32 = jnp.float32
 BF16 = jnp.bfloat16
@@ -151,7 +152,7 @@
         lax.fori_loop(1, self.nw, lambda k, n: (act(self.w_peer(k)), n)[1], 0)
 
     def reorder_to_w(self, dst, src, first):
-        step = self.slots // 2 if self.slots % 32 == 0 else self.slots
+        step = self.slots
         left = src[:, pl.ds(first, self.quarter)]
         right = src[:, pl.ds(first + self.quarter, self.quarter)]
 
@@ -184,7 +185,7 @@
     def turn_right(self):
         self.own(2).wait()
         self.each_w(lambda t: self.wc(1, self.w, t).wait_recv())
-        step = self.slots // 2 if self.slots % 32 == 0 else self.slots
+        step = self.slots
 
         def body(i, n):
             self.z1[at(i, step), :] = mm(self.to_z[at(i, step), :], self.r1[...]).astype(BF16)
@@ -291,6 +292,7 @@
     rows, depth = q_ref.shape
     slots = ndp * CAP
     tiles = depth // TILE
+    wides = depth // WIDE
     spot = (nz, nw, z, w, sub)
     ex = [
         Exchange(
@@ -341,7 +343,6 @@
             out[:, cols] = (ref[:, cols].astype(F32) / size).astype(BF16)
 
     unit(p_ref, pb, plen)
-    unit(q_ref, qb, qlen)
     pl.semaphore_wait(barrier, (nz - 1) + (nw - 1) + 2 * (SHIFTS - 1) + (ns - 1))
 
     def ask_z(to, frm):
@@ -368,16 +369,17 @@
         )
 
     along.each_z(lambda t: ask_z(t, z).start())
-    for side in range(2):
-        shift(0, side).start()
+    shift(0, 0).start()
+    unit(q_ref, qb, qlen)
+    shift(0, 1).start()
     ask1[at(z, nw), :] = ask0[at(z, nw), :]
 
     def logits(held):
         def body(i, total):
-            cols = at(i, TILE)
+            cols = at(i, WIDE)
             return total + mm_nt(qb[:, cols], held[:, cols])
 
-        return SHARPNESS * lax.fori_loop(0, tiles, body, jnp.zeros((rows, rows), F32))
+        return SHARPNESS * lax.fori_loop(0, wides, body, jnp.zeros((rows, rows), F32), unroll=True)
 
     along.each_z(lambda t: ask_z(z, t).wait_recv())
     ask2[...] = mm(swap[...], ask1[...].astype(BF16))
@@ -428,18 +430,17 @@
         shift(2, side).start()
     power[2] = jnp.exp(logits(ps.at[1]))
     ex[0].turn_right()
-    for side in range(2):
-        shift(2, side).wait_recv()
-    power[3] = jnp.exp(logits(ps.at[2]))
     ex[0].end_left()
     ex[0].end_right()
 
     def hard_logits(i, total):
-        cols = at(i, TILE)
+        cols = at(i, WIDE)
         return total + mm_nt(qb[:, cols], y1[:, cols])
 
-    hard = lax.fori_loop(0, tiles, hard_logits, jnp.zeros((rows, slots), F32))
+    hard = lax.fori_loop(0, wides, hard_logits, jnp.zeros((rows, slots), F32), unroll=True)
     hard = jnp.exp(SHARPNESS * hard) * gq[:, pl.ds(0, slots)]
+    shift(2, 0).wait_recv()
+    power[3] = jnp.exp(logits(ps.at[2]))
     totals = jnp.sum(hard, axis=1, keepdims=True)
     for k in range(SHIFTS):
         totals = totals + jnp.sum(power[k], axis=1, keepdims=True)
@@ -452,9 +453,9 @@
         x2[:, cols] = (SHARPNESS * mm(hard_t, qb[:, cols])).astype(BF16)
         return n
 
-    lax.fori_loop(0, half_tiles, slot_sums, 0)
+    lax.fori_loop(0, half_tiles, slot_sums, 0, unroll=True)
     ex[1].start_left()
-    lax.fori_loop(half_tiles, tiles, slot_sums, 0)
+    lax.fori_loop(half_tiles, tiles, slot_sums, 0, unroll=True)
     ex[1].start_right()
 
     def wt_copy(k):
@@ -505,30 +506,30 @@
         size = length[...]
 
         def radial(i, total):
-            cols = at(i, TILE)
+            cols = at(i, WIDE)
             return total + jnp.sum(
                 raw[:, cols].astype(F32) / size * grad[:, cols], axis=1, keepdims=True
             )
 
-        along_unit = lax.fori_loop(0, tiles, radial, jnp.zeros((rows, 1), F32))
+        along_unit = lax.fori_loop(0, wides, radial, jnp.zeros((rows, 1), F32), unroll=True)
 
         def write(i, n):
-            cols = at(i, TILE)
+            cols = at(i, WIDE)
             u = raw[:, cols].astype(F32) / size
             out[:, cols] = ((grad[:, cols] - u * along_unit) / size).astype(BF16)
             return n
 
-        lax.fori_loop(0, tiles, write, 0)
+        lax.fori_loop(0, wides, write, 0)
 
     def query_side(i, n):
-        cols = at(i, TILE)
+        cols = at(i, WIDE)
         total = mm(hard_w[...], y1[:, cols]) + mm(wrow[0], pb[:, cols])
         for k in range(1, SHIFTS):
             total = total + mm(wrow[k], ps[k - 1, :, cols])
         gq[:, cols] = SHARPNESS * total
         return n
 
-    lax.fori_loop(0, tiles, query_side, 0)
+    lax.fori_loop(0, wides, query_side, 0)
 
     along.each_z(lambda t: lz(z, t).wait_recv())
     l2[pl.ds(w, 1)] = ordered_sum(l1)[None]
@@ -536,38 +537,39 @@
 
     project(q_ref, qlen, gq, dq_ref)
 
-    ex[1].turn_left()
-
     for k in range(1, SHIFTS):
         wt_copy(k).wait_recv()
+    shift(2, 1).wait_recv()
 
     def passage_side(i, n):
-        cols = at(i, TILE)
+        cols = at(i, WIDE)
         total = mm(wt[0], qb[:, cols])
         for k in range(1, SHIFTS):
             total = total + mm(wt_in[k - 1], qs[k - 1, :, cols])
         gp[:, cols] = SHARPNESS * total
         return n
 
-    lax.fori_loop(0, tiles, passage_side, 0)
+    lax.fori_loop(0, wides, passage_side, 0)
+    ex[1].turn_left()
+    ex[1].turn_right()
+
     along.each_w(lambda t: lw(w, t).wait_recv())
     l3[pl.ds(sub, 1)] = ordered_sum(l2)[None]
     each_sub(lambda t: lsub(t, sub).start())
 
-    ex[1].turn_right()
 
     each_sub(lambda t: lsub(sub, t).wait_recv())
-    loss_ref[...] = ordered_sum(l3) / float(rows * ndp * ns)
-
-    ex[1].end_left()
-    ex[1].end_right()
+    loss_ref[...] = (ordered_sum(l3) / float(rows * ndp * ns))[0:1, 0:1]
 
     def add_returned(i, n):
         cols = at(i, TILE)
         gp[:, cols] = gp[:, cols] + mm(pick_t[...], y2[:, cols])
         return n
 
-    lax.fori_loop(0, tiles, add_returned, 0)
+    ex[1].end_left()
+    lax.fori_loop(0, half_tiles, add_returned, 0, unroll=True)
+    ex[1].end_right()
+    lax.fori_loop(half_tiles, tiles, add_returned, 0, unroll=True)
     project(p_ref, plen, gp, dp_ref)
 
     along.each_z(lambda t: ask_z(t, z).wait_send())
@@ -628,7 +630,7 @@
         out_shape=(
             jax.ShapeDtypeStruct((rows, depth), BF16),
             jax.ShapeDtypeStruct((rows, depth), BF16),
-            jax.ShapeDtypeStruct((8, 128), F32),
+            jax.ShapeDtypeStruct((1, 1), F32),
         ),
         in_specs=[vmem] * (5 + len(fixed)),
         out_specs=(vmem, vmem, vmem),
@@ -640,7 +642,7 @@
             flops=flops, bytes_accessed=12 * rows * depth, transcendentals=rows * slots * 2
         ),
     )(queries, passages, requests, counts, neg_slot, *fixed)
-    return dq, dp, loss[0, 0]
+    return dq, dp, loss.reshape(())
 
 
 def solution(mesh):

time: 261 us -> 244 us (0.935)
  the two profiles are of different devices: /device:TPU:25 before, /device:TPU:1 now
where the time goes in v2:
time: 244 us
  Pallas kernels  235 us (96%)
  local copies, waits for them, and re-layouts  6 us (2%)
  between operations  2.47 us (1%)
    pallas_call x1, Pallas kernels, on_device(): pl.pallas_call(functools.partial(kernel, nz, nw, ns), out_shape=(jax.Shap...  235 us
    unnamed x6, local copies, waits for them, and re-layouts  6 us

profile of v2, /device:TPU:1, one launch (start us, length us, event | category | flops | bytes accessed | tf_op | source)
XLA Modules:
  0.0 243.7 jit_solution(1525855187730501828)
XLA Ops:
  0.6 1.4 copy.16.req_ref
  2.0 1.4 copy.17.neg_ref
  3.5 235.2 %shard_map.148 = (bf16[128,3584]{1,0:T(8,128)(2,1)}, bf16[128,3584]{1,0:T(8,128)(2,1)}, f32[1,1]{1,0:T(1,128)}) custom-call(bf16[128,3584]{1,0:T(8,128)(2,1)} %q_ref.1, bf16[128,3584]{1,0:T(8,128)(2,1)} %p_ref.1, s32[1,128,3]{2,1,0:T(8,128)} %copy.16.req_ref, s32[1,128]{1,0:T(1,128)} %cnt_ref.1, s32[128,7]{1,0:T(8,128)} %copy.17.neg_ref, ...), custom_call_target="tpu_custom_call" | custom-call | flops 10569646080 | bytes 5505024 | tf_op jit(solution)/shard_map/pallas_call | solution.py:628
  238.7 0.0 copy-start
  238.7 2.2 copy.21
  240.9 0.0 copy-done
  241.0 0.9 copy.22
Async XLA Ops:
  238.7 2.3 copy-start

commit v3 on v2

--- a/solution.py
+++ b/solution.py
@@ -431,13 +431,14 @@
     power[2] = jnp.exp(logits(ps.at[1]))
     ex[0].turn_right()
     ex[0].end_left()
+
+    def hard_logits(i, total):
+        cols = at(i, depth // 4)
+        return total + mm_nt(qb[:, cols], y1[:, cols])
+
+    hard = lax.fori_loop(0, 2, hard_logits, jnp.zeros((rows, slots), F32), unroll=True)
     ex[0].end_right()
-
-    def hard_logits(i, total):
-        cols = at(i, WIDE)
-        return total + mm_nt(qb[:, cols], y1[:, cols])
-
-    hard = lax.fori_loop(0, wides, hard_logits, jnp.zeros((rows, slots), F32), unroll=True)
+    hard = lax.fori_loop(2, 4, hard_logits, hard, unroll=True)
     hard = jnp.exp(SHARPNESS * hard) * gq[:, pl.ds(0, slots)]
     shift(2, 0).wait_recv()
     power[3] = jnp.exp(logits(ps.at[2]))

time: 244 us -> 244 us (level)
  no operation moved by 1% of the time
where the time goes in v3:
time: 244 us
  Pallas kernels  235 us (96%)
  local copies, waits for them, and re-layouts  6 us (2%)
  between operations  2.47 us (1%)
    pallas_call x1, Pallas kernels, on_device(): pl.pallas_call(functools.partial(kernel, nz, nw, ns), out_shape=(jax.Shap...  235 us
    unnamed x6, local copies, waits for them, and re-layouts  6 us

profile of v3, /device:TPU:1, one launch (start us, length us, event | category | flops | bytes accessed | tf_op | source)
XLA Modules:
  0.0 243.7 jit_solution(8696710461476083961)
XLA Ops:
  0.6 1.4 copy.16.req_ref
  2.0 1.4 copy.17.neg_ref
  3.5 235.2 %shard_map.148 = (bf16[128,3584]{1,0:T(8,128)(2,1)}, bf16[128,3584]{1,0:T(8,128)(2,1)}, f32[1,1]{1,0:T(1,128)}) custom-call(bf16[128,3584]{1,0:T(8,128)(2,1)} %q_ref.1, bf16[128,3584]{1,0:T(8,128)(2,1)} %p_ref.1, s32[1,128,3]{2,1,0:T(8,128)} %copy.16.req_ref, s32[1,128]{1,0:T(1,128)} %cnt_ref.1, s32[128,7]{1,0:T(8,128)} %copy.17.neg_ref, ...), custom_call_target="tpu_custom_call" | custom-call | flops 10569646080 | bytes 5505024 | tf_op jit(solution)/shard_map/pallas_call | solution.py:629
  238.7 0.0 copy-start
  238.7 2.2 copy.21
  240.9 0.0 copy-done
  240.9 0.9 copy.22
Async XLA Ops:
  238.7 2.3 copy-start
